TPU v7x, 256 devices: a whole 4x4x8 slice. The times are simulated.
256 devices in a mesh: pipe: 16 (over x_lo, y, core), expert: 8 (over z), dp: 2 (over x_hi).
Axes of the slice: x: 4 (x_hi: 2, x_lo: 2; x = x_hi * 2 + x_lo), y: 4, z: 8, core: 2. Of those that a mesh axis runs over, the one named last changes fastest.
Arguments:
- fwd_in: bfloat16 [16, 2048, 3584], P('pipe', ('expert', 'dp')), may hold values from -6 to 6
- fwd_ids: int32 [16, 2048, 1], P('pipe', ('expert', 'dp')), may hold values from 0 to 3; in each aligned block of 128 rows (0 to 127, 128 to 255, ..., all dimensions but the last counted through in order) at most 40 rows name the same one
- fwd_gates: float32 [16, 2048, 1], P('pipe', ('expert', 'dp')), may hold values from 0.2 to 1
- bwd_in: bfloat16 [16, 2048, 3584], P('pipe', ('expert', 'dp')), may hold values from -6 to 6
- bwd_grad: bfloat16 [16, 2048, 3584], P('pipe', ('expert', 'dp')), may hold values from -6 to 6
- bwd_ids: int32 [16, 2048, 1], P('pipe', ('expert', 'dp')), may hold values from 0 to 3; in each aligned block of 128 rows (0 to 127, 128 to 255, ..., all dimensions but the last counted through in order) at most 40 rows name the same one
- bwd_gates: float32 [16, 2048, 1], P('pipe', ('expert', 'dp')), may hold values from 0.2 to 1
- gate_w: bfloat16 [16, 3584, 4096], P('pipe', 'dp', 'expert'), may hold values from -0.09375 to 0.09375
- up_w: bfloat16 [16, 3584, 4096], P('pipe', 'dp', 'expert'), may hold values from -0.09375 to 0.09375
- down_w: bfloat16 [16, 3584, 4096], P('pipe', 'dp', 'expert'), may hold values from -0.1875 to 0.1875
Outputs:
- fwd_next: bfloat16 [16, 2048, 3584], P('pipe', ('expert', 'dp'))
- bwd_next: bfloat16 [16, 2048, 3584], P('pipe', ('expert', 'dp'))
- gate_grad: bfloat16 [16, 3584, 4096], P('pipe', 'dp', 'expert')
Inputs may be any that keep to these rules, and one draw needn't show every extreme that they name: `fwd_ids`: at every section the 128 tokens of one routing block (aligned blocks of rows) name any expert at most 40 times, a bound that some block reaches; each token names exactly 1 expert. `bwd_ids`: as for fwd_ids.
All inputs are finite; a program needn't handle non-finite values.
Results may differ from a plain program's by a relative error of at most 0.01.
Values may be sent and summed in bfloat16 or wider, within the bound.
A program may use at most 128 MiB of HBM per device.

v0:
```python
import jax
import jax.numpy as jnp
from jax import lax
from jax.sharding import PartitionSpec as P

SPLIT = 2


def shifted(block, axis, distance):
    devices = range(lax.axis_size(axis))
    route = [((i - distance) % len(devices), i) for i in devices]
    return lax.ppermute(block, axis, route)


def slot_index(ids, experts, capacity):
    flat = ids.reshape(-1)
    onehot = (flat[:, None] == jnp.arange(experts, dtype=jnp.int32)[None, :]).astype(jnp.int32)
    ranked = jnp.sum(onehot * (jnp.cumsum(onehot, axis=0) - 1), axis=1)
    return flat * capacity + ranked


def dispatch(rows, index, experts, capacity):
    empty = jnp.zeros((experts * capacity, rows.shape[1]), rows.dtype)
    placed = empty.at[index].set(rows).reshape(experts, capacity, rows.shape[1])
    return jnp.repeat(placed, SPLIT, axis=0)


def merge_halves(returned, experts):
    shape = returned.shape
    parts = returned.reshape(experts, SPLIT, shape[1], shape[2]).astype(jnp.float32)
    return jnp.sum(parts, axis=1)


def collect(output, index, gates, base):
    picked = output.reshape(-1, output.shape[2])[index].reshape(gates.shape[0], gates.shape[1], -1)
    total = base.astype(jnp.float32) + jnp.sum(gates[:, :, None] * picked, axis=1)
    return total.astype(jnp.bfloat16)


def expert_forward(received, w_gate, w_up, w_down):
    shape = received.shape
    rows = received.reshape(-1, shape[2])
    gate_pre = jnp.dot(rows, w_gate, preferred_element_type=jnp.float32)
    up_pre = jnp.dot(rows, w_up, preferred_element_type=jnp.float32)
    hidden = (jax.nn.silu(gate_pre) * up_pre).astype(jnp.bfloat16)
    output = lax.dot_general(
        hidden, w_down, (((1,), (1,)), ((), ())), preferred_element_type=jnp.float32
    )
    return output.astype(jnp.bfloat16).reshape(shape)


def expert_backward(x_recv, z_recv, w_gate, w_up, w_down):
    shape = x_recv.shape
    x_rows = x_recv.reshape(-1, shape[2])
    z_rows = z_recv.reshape(-1, shape[2])
    gate_pre = jnp.dot(x_rows, w_gate, preferred_element_type=jnp.float32)
    up_pre = jnp.dot(x_rows, w_up, preferred_element_type=jnp.float32)
    sigma = jax.nn.sigmoid(gate_pre)
    active = gate_pre * sigma
    d_hidden = jnp.dot(z_rows, w_down, preferred_element_type=jnp.float32)
    d_gate = (d_hidden * up_pre * sigma * (1.0 + gate_pre * (1.0 - sigma))).astype(jnp.bfloat16)
    d_up = (d_hidden * active).astype(jnp.bfloat16)
    contract = (((1,), (1,)), ((), ()))
    back = lax.dot_general(d_gate, w_gate, contract, preferred_element_type=jnp.float32)
    back = back + lax.dot_general(d_up, w_up, contract, preferred_element_type=jnp.float32)
    inner = (shape[0], shape[1], w_gate.shape[1])
    return (back.astype(jnp.bfloat16).reshape(shape), d_gate.reshape(inner))


def per_device(
    fwd_in, fwd_ids, fwd_gates, bwd_in, bwd_grad, bwd_ids, bwd_gates, gate_w, up_w, down_w
):
    holders = lax.axis_size("expert")
    experts = holders // SPLIT
    w_gate, w_up, w_down = (
        lax.all_gather(gate_w[0], "dp", axis=0, tiled=True),
        lax.all_gather(up_w[0], "dp", axis=0, tiled=True),
        lax.all_gather(down_w[0], "dp", axis=0, tiled=True),
    )
    f_rows = fwd_in[0]
    x_rows_in = bwd_in[0]
    g_rows = bwd_grad[0]
    row_count = f_rows.shape[0]
    features = f_rows.shape[1]
    picks = fwd_ids.shape[2]
    capacity = min(row_count, row_count * picks * 5 // (4 * experts))
    f_index = slot_index(fwd_ids[0], experts, capacity)
    f_buf = dispatch(jnp.repeat(f_rows, picks, axis=0), f_index, experts, capacity)
    b_index = slot_index(bwd_ids[0], experts, capacity)
    scaled = (bwd_gates[0][:, :, None] * g_rows[:, None, :].astype(jnp.float32)).astype(
        jnp.bfloat16
    )
    x_buf = dispatch(jnp.repeat(x_rows_in, picks, axis=0), b_index, experts, capacity)
    z_buf = dispatch(scaled.reshape(-1, features), b_index, experts, capacity)
    received = lax.all_to_all(f_buf, "expert", split_axis=0, concat_axis=0, tiled=True)
    f_back = lax.all_to_all(
        expert_forward(received, w_gate, w_up, w_down),
        "expert",
        split_axis=0,
        concat_axis=0,
        tiled=True,
    )
    x_recv, z_recv = (
        lax.all_to_all(x_buf, "expert", split_axis=0, concat_axis=0, tiled=True),
        lax.all_to_all(z_buf, "expert", split_axis=0, concat_axis=0, tiled=True),
    )
    back, d_gate = expert_backward(x_recv, z_recv, w_gate, w_up, w_down)
    b_back = lax.all_to_all(back, "expert", split_axis=0, concat_axis=0, tiled=True)
    layer_out = collect(merge_halves(f_back, experts), f_index, fwd_gates[0], f_rows)
    input_grad = collect(
        merge_halves(b_back, experts), b_index, jnp.ones_like(bwd_gates[0]), g_rows
    )
    fwd_next = shifted(layer_out[None], "pipe", 1)
    bwd_next = shifted(input_grad[None], "pipe", -1)
    hidden_units = w_gate.shape[1]
    x_rows = x_recv.reshape(-1, features)
    gate_rows = d_gate.reshape(-1, hidden_units)
    contract = (((0,), (0,)), ((), ()))
    summed = lax.psum_scatter(
        lax.dot_general(x_rows, gate_rows, contract, preferred_element_type=jnp.float32).astype(
            jnp.bfloat16
        ),
        "dp",
        scatter_dimension=0,
        tiled=True,
    )
    gate_grad = summed[None]
    return (fwd_next, bwd_next, gate_grad)


def solution(mesh):
    return jax.shard_map(
        per_device,
        mesh=mesh,
        in_specs=(
            P("pipe", ("expert", "dp"), None),
            P("pipe", ("expert", "dp"), None),
            P("pipe", ("expert", "dp"), None),
            P("pipe", ("expert", "dp"), None),
            P("pipe", ("expert", "dp"), None),
            P("pipe", ("expert", "dp"), None),
            P("pipe", ("expert", "dp"), None),
            P("pipe", "dp", "expert"),
            P("pipe", "dp", "expert"),
            P("pipe", "dp", "expert"),
        ),
        out_specs=(
            P("pipe", ("expert", "dp"), None),
            P("pipe", ("expert", "dp"), None),
            P("pipe", "dp", "expert"),
        ),
        check_vma=False,
    )
```

profile of v0, /device:TPU:1, one launch (start us, length us, event | category | flops | bytes accessed | tf_op | source)
XLA Modules:
  0.0 348.3 jit_solution(5725379315154069737)
XLA Ops:
  7.2 0.0 copy-start
  7.2 0.0 copy-start.5
  7.2 0.0 all-gather.7.cloned.1.call-start
  7.2 0.7 all-gather.7.cloned.1.call-update
  7.9 0.7 fusion.53
  8.7 0.2 reduce_window_sum.17
  8.8 0.8 select_reduce_fusion.1
  9.7 0.7 fusion.54
  10.3 2.2 scatter_custom_fusion
  12.5 1.7 broadcast_in_dim.8
  14.2 9.1 %all-to-all-start = ((bf16[8,40,3584]{2,1,0:T(8,128)(2,1)}), bf16[8,40,3584]{2,1,0:T(8,128)(2,1)}, u32[]{:S(2)}, u32[]{:S(2)}) async-start(bf16[8,40,3584]{2,1,0:T(8,128)(2,1)} %bitcast.7), calls=%async_computation | async-start | bytes 4587520 | tf_op jit(solution)/shard_map/all_to_all | solution.py:95
  23.4 0.0 all-gather.11.cloned.1.call-start
  23.4 0.7 all-gather.11.cloned.1.call-update
  24.1 0.0 copy-done.13
  24.1 0.1 fusion.52
  24.2 0.2 reduce_window_sum.18
  24.4 0.2 select_reduce_fusion
  24.6 2.3 scatter_custom_fusion.1
  26.8 49.4 %all-to-all-done = bf16[8,40,3584]{2,1,0:T(8,128)(2,1)} async-done(((bf16[8,40,3584]{2,1,0:T(8,128)(2,1)}), bf16[8,40,3584]{2,1,0:T(8,128)(2,1)}, u32[]{:S(2)}, u32[]{:S(2)}) %all-to-all-start) | async-done | bytes 2293792 | tf_op jit(solution)/shard_map/all_to_all | solution.py:95
  76.3 1.7 broadcast_in_dim.9
  77.9 4.4 %all-to-all-start.2 = ((bf16[8,40,3584]{2,1,0:T(8,128)(2,1)}), bf16[8,40,3584]{2,1,0:T(8,128)(2,1)}, u32[]{:S(2)}, u32[]{:S(2)}) async-start(bf16[8,40,3584]{2,1,0:T(8,128)(2,1)} %bitcast.23), calls=%async_computation.2 | async-start | bytes 4587520 | tf_op jit(solution)/shard_map/all_to_all | solution.py:105
  82.3 0.0 all-gather.9.cloned.1.call-start
  82.4 0.7 all-gather.9.cloned.1.call-update
  83.1 2.2 scatter_custom_fusion.2
  85.3 50.5 %all-to-all-done.2 = bf16[8,40,3584]{2,1,0:T(8,128)(2,1)} async-done(((bf16[8,40,3584]{2,1,0:T(8,128)(2,1)}), bf16[8,40,3584]{2,1,0:T(8,128)(2,1)}, u32[]{:S(2)}, u32[]{:S(2)}) %all-to-all-start.2) | async-done | bytes 2293792 | tf_op jit(solution)/shard_map/all_to_all | solution.py:105
  135.8 1.5 broadcast_in_dim.10
  137.3 3.6 %all-to-all-start.3 = ((bf16[8,40,3584]{2,1,0:T(8,128)(2,1)}), bf16[8,40,3584]{2,1,0:T(8,128)(2,1)S(1)}, u32[]{:S(2)}, u32[]{:S(2)}) async-start(bf16[8,40,3584]{2,1,0:T(8,128)(2,1)} %bitcast.27), calls=%async_computation.3 | async-start | bytes 4587520 | tf_op jit(solution)/shard_map/all_to_all | solution.py:104
  140.9 0.0 all-gather.7.cloned.1.call-done
  141.0 4.5 %fusion.13 = f32[320,512]{1,0:T(8,128)S(1)} fusion(bf16[320,3584]{1,0:T(8,128)(2,1)} %bitcast.8, bf16[1,3584,512]{2,1,0:T(8,128)(2,1)} %all-gather.7.cloned.1.call-done), kind=kOutput, calls=%fused_computation.23 | convolution fusion | flops 1174405120 | bytes 6619136 | tf_op jit(solution)/shard_map/dot_general | solution.py:43
  145.5 0.0 all-gather.11.cloned.1.call-done
  145.5 43.1 %all-gather.9.cloned.1.call-done = bf16[1,3584,512]{2,1,0:T(8,128)(2,1)} async-done(((bf16[1,1792,512]{2,1,0:T(8,128)(2,1)}), bf16[1,3584,512]{2,1,0:T(8,128)(2,1)}) %all-gather.9.cloned.1.call-update) | async-done | bytes 3670032 | tf_op jit(solution)/shard_map/all_gather | solution.py:77
  188.6 7.9 %convolution_convert_fusion.1 = bf16[320,3584]{1,0:T(8,128)(2,1)} fusion(bf16[1,3584,512]{2,1,0:T(8,128)(2,1)} %all-gather.11.cloned.1.call-done, bf16[320,3584]{1,0:T(8,128)(2,1)} %bitcast.8, bf16[1,3584,512]{2,1,0:T(8,128)(2,1)} %all-gather.9.cloned.1.call-done, f32[320,512]{1,0:T(8,128)S(1)} %fusion.13), kind=kOutput, calls=%fused_computation.8 | convolution fusion | flops 2350940160 | bytes 12582912 | tf_op jit(solution)/shard_map/dot_general | solution.py:46
  196.6 0.1 all-to-all-done.3
  196.7 1.4 copy-done.9
  198.1 6.5 %all-to-all-start.1 = ((bf16[8,40,3584]{2,1,0:T(8,128)(2,1)}), bf16[8,40,3584]{2,1,0:T(8,128)(2,1)S(1)}, u32[]{:S(2)}, u32[]{:S(2)}) async-start(bf16[8,40,3584]{2,1,0:T(8,128)(2,1)} %bitcast.107), calls=%async_computation.1 | async-start | bytes 4587520 | tf_op jit(solution)/shard_map/all_to_all | solution.py:96
  204.6 0.2 reduce-scatter.2.cloned.1.call-start
  204.9 4.2 %fusion.1 = f32[320,512]{1,0:T(8,128)S(1)} fusion(bf16[320,3584]{1,0:T(8,128)(2,1)} %bitcast.24, bf16[1,3584,512]{2,1,0:T(8,128)(2,1)} %all-gather.11.cloned.1.call-done), kind=kOutput, calls=%fused_computation.11 | convolution fusion | flops 1174405120 | bytes 6619136 | tf_op jit(solution)/shard_map/dot_general | solution.py:60
  209.1 0.3 copy-done.10
  209.4 1.3 fusion.11
  210.7 0.7 copy-done.7
  211.4 1.5 fusion.32
  212.9 4.0 %convolution_convert_fusion = bf16[3584,512]{1,0:T(8,128)(2,1)} fusion(bf16[320,3584]{1,0:T(8,128)(2,1)S(1)} %bitcast.110, bf16[320,512]{1,0:T(8,128)(2,1)S(1)} %fusion.32), kind=kOutput, calls=%fused_computation.5 | convolution fusion | flops 1176240128 | bytes 6291456 | tf_op jit(solution)/shard_map/dot_general | solution.py:120
  216.9 0.0 reduce-scatter.2.cloned.1.call-update
  216.9 0.0 copy-start.12
  216.9 3.6 %fusion.9 = f32[320,3584]{1,0:T(8,128)S(1)} fusion(bf16[320,512]{1,0:T(8,128)(2,1)S(1)} %fusion.32, bf16[1,3584,512]{2,1,0:T(8,128)(2,1)} %all-gather.7.cloned.1.call-done), kind=kOutput, calls=%fused_computation.19 | convolution fusion | flops 1174405120 | bytes 8585216 | tf_op jit(solution)/shard_map/dot_general | solution.py:64
  220.5 2.8 fusion
  223.3 34.1 %all-to-all-done.1 = bf16[8,40,3584]{2,1,0:T(8,128)(2,1)S(1)} async-done(((bf16[8,40,3584]{2,1,0:T(8,128)(2,1)}), bf16[8,40,3584]{2,1,0:T(8,128)(2,1)S(1)}, u32[]{:S(2)}, u32[]{:S(2)}) %all-to-all-start.1) | async-done | bytes 2293792 | tf_op jit(solution)/shard_map/all_to_all | solution.py:96
  257.4 1.4 copy-done.2
  258.8 4.4 %all-to-all-start.4 = ((bf16[8,40,3584]{2,1,0:T(8,128)(2,1)}), bf16[8,40,3584]{2,1,0:T(8,128)(2,1)}, u32[]{:S(2)}, u32[]{:S(2)}) async-start(bf16[8,40,3584]{2,1,0:T(8,128)(2,1)} %bitcast.29), calls=%async_computation.4 | async-start | bytes 4587520 | tf_op jit(solution)/shard_map/all_to_all | solution.py:108
  263.2 2.3 convert_reduce_fusion.1
  265.5 0.0 copy-start.6
  265.5 0.0 copy-start.15
  265.5 2.4 gather_fusion
  267.9 2.7 fusion.19
  270.6 4.7 %collective-permute-start = (bf16[1,128,3584]{2,1,0:T(8,128)(2,1)}, bf16[1,128,3584]{2,1,0:T(8,128)(2,1)}, u32[]{:S(2)}, u32[]{:S(2)}) collective-permute-start(bf16[1,128,3584]{2,1,0:T(8,128)(2,1)} %fusion.19), channel_id=1, source_target_pairs={{240,0},{0,16},{16,32},{32,48},{48,64},{64,80},{80,96},{96,112},{1... | collective-permute-start | bytes 2752520 | tf_op jit(solution)/shard_map/ppermute | solution.py:12
  275.3 41.4 %all-to-all-done.4 = bf16[8,40,3584]{2,1,0:T(8,128)(2,1)} async-done(((bf16[8,40,3584]{2,1,0:T(8,128)(2,1)}), bf16[8,40,3584]{2,1,0:T(8,128)(2,1)}, u32[]{:S(2)}, u32[]{:S(2)}) %all-to-all-start.4) | async-done | bytes 2293792 | tf_op jit(solution)/shard_map/all_to_all | solution.py:108
  316.7 2.3 convert_reduce_fusion
  319.0 2.4 gather_fusion.1
  321.4 2.0 fusion.15
  323.4 3.1 collective-permute-start.1
  326.5 0.0 collective-permute-done
  326.5 12.2 %collective-permute-done.1 = bf16[1,128,3584]{2,1,0:T(8,128)(2,1)S(1)} collective-permute-done((bf16[1,128,3584]{2,1,0:T(8,128)(2,1)S(1)}, bf16[1,128,3584]{2,1,0:T(8,128)(2,1)S(1)}, u32[]{:S(2)}, u32[]{:S(2)}) %collective-permute-start.1) | collective-permute-done | bytes 917536 | tf_op jit(solution)/shard_map/ppermute | solution.py:12
  338.7 2.2 copy.15
  340.9 0.9 copy.16
  (26 shorter events, 0.1 us)
Async XLA Ops:
  7.2 75.9 %copy-start = (bf16[1,128,3584]{2,1,0:T(8,128)(2,1)S(1)}, bf16[1,128,3584]{2,1,0:T(8,128)(2,1)}, u32[]{:S(2)}) copy-start(bf16[1,128,3584]{2,1,0:T(8,128)(2,1)} %param.13) | copy-start | bytes 2752516
  7.2 3.2 copy-start.5
  7.2 133.8 %all-gather.7.cloned.1.call-start = ((), (), s32[]{:S(2)}) async-start(), calls=%async_computation.7 | async-start | bytes 5505024 | tf_op jit(solution)/shard_map/all_gather | solution.py:76
  14.2 9.9 %copy-start.13 = (s32[1,128,1]{1,2,0:T(1,128)S(1)}, s32[1,128,1]{1,2,0:T(1,128)}, u32[]{:S(2)}) copy-start(s32[1,128,1]{1,2,0:T(1,128)} %param.15) | copy-start | bytes 1540
  14.2 10.4 %copy-start.3 = (bf16[1,128,3584]{2,1,0:T(8,128)(2,1)S(1)}, bf16[1,128,3584]{2,1,0:T(8,128)(2,1)}, u32[]{:S(2)}) copy-start(bf16[1,128,3584]{2,1,0:T(8,128)(2,1)} %param.14) | copy-start | bytes 2752516
  14.2 10.4 %copy-start.14 = (f32[1,128,1]{1,2,0:T(1,128)S(1)}, f32[1,128,1]{1,2,0:T(1,128)}, u32[]{:S(2)}) copy-start(f32[1,128,1]{1,2,0:T(1,128)} %param.16) | copy-start | bytes 1540
  14.2 62.1 %all-to-all-start = ((bf16[8,40,3584]{2,1,0:T(8,128)(2,1)}), bf16[8,40,3584]{2,1,0:T(8,128)(2,1)}, u32[]{:S(2)}, u32[]{:S(2)}) async-start(bf16[8,40,3584]{2,1,0:T(8,128)(2,1)} %bitcast.7), calls=%async_computation | async-start | bytes 4587520 | tf_op jit(solution)/shard_map/all_to_all | solution.py:95
  23.4 122.2 %all-gather.11.cloned.1.call-start = ((), (), s32[]{:S(2)}) async-start(), calls=%async_computation.9 | async-start | bytes 5505024 | tf_op jit(solution)/shard_map/all_gather | solution.py:78
  77.9 57.9 %all-to-all-start.2 = ((bf16[8,40,3584]{2,1,0:T(8,128)(2,1)}), bf16[8,40,3584]{2,1,0:T(8,128)(2,1)}, u32[]{:S(2)}, u32[]{:S(2)}) async-start(bf16[8,40,3584]{2,1,0:T(8,128)(2,1)} %bitcast.23), calls=%async_computation.2 | async-start | bytes 4587520 | tf_op jit(solution)/shard_map/all_to_all | solution.py:105
  82.3 106.3 %all-gather.9.cloned.1.call-start = ((), (), s32[]{:S(2)}) async-start(), calls=%async_computation.8 | async-start | bytes 5505024 | tf_op jit(solution)/shard_map/all_gather | solution.py:77
  137.3 59.4 %all-to-all-start.3 = ((bf16[8,40,3584]{2,1,0:T(8,128)(2,1)}), bf16[8,40,3584]{2,1,0:T(8,128)(2,1)S(1)}, u32[]{:S(2)}, u32[]{:S(2)}) async-start(bf16[8,40,3584]{2,1,0:T(8,128)(2,1)} %bitcast.27), calls=%async_computation.3 | async-start | bytes 4587520 | tf_op jit(solution)/shard_map/all_to_all | solution.py:104
  196.7 1.4 copy-start.9
  198.1 59.4 %all-to-all-start.1 = ((bf16[8,40,3584]{2,1,0:T(8,128)(2,1)}), bf16[8,40,3584]{2,1,0:T(8,128)(2,1)S(1)}, u32[]{:S(2)}, u32[]{:S(2)}) async-start(bf16[8,40,3584]{2,1,0:T(8,128)(2,1)} %bitcast.107), calls=%async_computation.1 | async-start | bytes 4587520 | tf_op jit(solution)/shard_map/all_to_all | solution.py:96
  204.6 134.1 %reduce-scatter.2.cloned.1.call-start = ((), (), s32[]{:S(2)}) async-start(), calls=%async_computation.6 | async-start | bytes 5505024 | tf_op jit(solution)/shard_map/reduce_scatter | solution.py:119
  204.9 4.2 %copy-start.4 = (bf16[1,3584,512]{2,1,0:T(8,128)(2,1)S(1)}, bf16[1,3584,512]{2,1,0:T(8,128)(2,1)}, u32[]{:S(2)}) copy-start(bf16[1,3584,512]{2,1,0:T(8,128)(2,1)} %all-gather.7.cloned.1.call-done) | copy-start | bytes 11010052
  204.9 4.5 %copy-start.10 = (bf16[8,40,3584]{2,1,0:T(8,128)(2,1)S(1)}, bf16[8,40,3584]{2,1,0:T(8,128)(2,1)}, u32[]{:S(2)}) copy-start(bf16[8,40,3584]{2,1,0:T(8,128)(2,1)} %copy-done.9) | copy-start | bytes 6881284
  209.4 2.0 copy-start.7
  211.4 1.5 copy-start.11
  216.9 3.6 %copy-start.8 = (bf16[1,3584,512]{2,1,0:T(8,128)(2,1)S(1)}, bf16[1,3584,512]{2,1,0:T(8,128)(2,1)}, u32[]{:S(2)}) copy-start(bf16[1,3584,512]{2,1,0:T(8,128)(2,1)} %all-gather.9.cloned.1.call-done) | copy-start | bytes 11010052
  216.9 3.6 %copy-start.12 = (f32[320,512]{1,0:T(8,128)S(1)}, f32[320,512]{1,0:T(8,128)}, u32[]{:S(2)}) copy-start(f32[320,512]{1,0:T(8,128)} %copy-done.11) | copy-start | bytes 1966084
  257.4 1.4 copy-start.2
  258.8 57.9 %all-to-all-start.4 = ((bf16[8,40,3584]{2,1,0:T(8,128)(2,1)}), bf16[8,40,3584]{2,1,0:T(8,128)(2,1)}, u32[]{:S(2)}, u32[]{:S(2)}) async-start(bf16[8,40,3584]{2,1,0:T(8,128)(2,1)} %bitcast.29), calls=%async_computation.4 | async-start | bytes 4587520 | tf_op jit(solution)/shard_map/all_to_all | solution.py:108
  265.5 2.4 copy-start.6
  265.5 2.4 copy-start.15
  270.6 55.9 %collective-permute-start = (bf16[1,128,3584]{2,1,0:T(8,128)(2,1)}, bf16[1,128,3584]{2,1,0:T(8,128)(2,1)}, u32[]{:S(2)}, u32[]{:S(2)}) collective-permute-start(bf16[1,128,3584]{2,1,0:T(8,128)(2,1)} %fusion.19), channel_id=1, source_target_pairs={{240,0},{0,16},{16,32},{32,48},{48,64},{64,80},{80,96},{96,112},{1... | collective-permute-start | bytes 2752520 | tf_op jit(solution)/shard_map/ppermute | solution.py:12
  321.4 20.4 %copy-start.1 = (bf16[1,128,3584]{2,1,0:T(8,128)(2,1)S(1)}, bf16[1,128,3584]{2,1,0:T(8,128)(2,1)}, u32[]{:S(2)}) copy-start(bf16[1,128,3584]{2,1,0:T(8,128)(2,1)} %param.13) | copy-start | bytes 2752516
  323.4 15.3 %collective-permute-start.1 = (bf16[1,128,3584]{2,1,0:T(8,128)(2,1)S(1)}, bf16[1,128,3584]{2,1,0:T(8,128)(2,1)S(1)}, u32[]{:S(2)}, u32[]{:S(2)}) collective-permute-start(bf16[1,128,3584]{2,1,0:T(8,128)(2,1)S(1)} %fusion.15), channel_id=1, source_target_pairs={{16,0},{32,16},{48,32},{64,48},{80,64},{96,80},{112,96},{128,112},... | collective-permute-start | bytes 2752520 | tf_op jit(solution)/shard_map/ppermute | solution.py:12
Sparse Core Ops, SparseCore 0:
  9.8 61.2 all-gather.6
  72.9 56.9 all-gather.10
  131.7 56.9 all-gather.8
  217.0 55.4 reduce-scatter.1
where the time goes:
time: 349 us; the launch traced here: 348 us
  waiting for transfers between devices  233 us (67%)
  starting transfers between devices  36.2 us (10%)
  matrix products  29.8 us (9%)
  local copies, waits for them, and re-layouts  20.9 us (6%)
  other arithmetic  14.3 us (4%)
  between operations  14 us (4%)
    all_to_all x1, waiting for transfers between devices, per_device(): lax.all_to_all(z_buf, 'expert', split_axis=0, concat_axis=0, tiled=True)  50.5 us
    all_to_all x1, waiting for transfers between devices, per_device(): lax.all_to_all(f_buf, 'expert', split_axis=0, concat_axis=0, tiled=True)  49.4 us
    all_gather x1, waiting for transfers between devices, per_device(): lax.all_gather(up_w[0], 'dp', axis=0, tiled=True)  43.1 us
    all_to_all x1, waiting for transfers between devices, per_device(): lax.all_to_all(back, 'expert', split_axis=0, concat_axis=0, tiled=True)  41.4 us
    all_to_all x1, waiting for transfers between devices, per_device(): lax.all_to_all(expert_forward(received, w_gate, w_up, w_down), 'expert',...  34.1 us
    ppermute x2, waiting for transfers between devices, shifted(): return lax.ppermute(block, axis, route)  12.2 us
    all_to_all x1, starting transfers between devices, per_device(): lax.all_to_all(f_buf, 'expert', split_axis=0, concat_axis=0, tiled=True)  9.15 us
    dot_general x1, matrix products, expert_forward(): lax.dot_general(hidden, w_down, (((1,), (1,)), ((), ())), preferred_eleme...  7.94 us
  transfers between devices with their start and end apart: 11, of which 7 were waited for; matrix products, arithmetic and copies ran while one was open for 17% of the time, Pallas kernels for 0%

commit v1 on v0

--- a/solution.py
+++ b/solution.py
@@ -74,7 +74,9 @@
     experts = holders // SPLIT
     w_gate, w_up, w_down = (
         lax.all_gather(gate_w[0], "dp", axis=0, tiled=True),
-        lax.all_gather(up_w[0], "dp", axis=0, tiled=True),
+        jnp.concatenate(
+            lax.all_to_all(jnp.stack([up_w[0]] * lax.axis_size("dp")), "dp", 0, 0), axis=0
+        ),
         lax.all_gather(down_w[0], "dp", axis=0, tiled=True),
     )
     f_rows = fwd_in[0]

time: 349 us -> 397 us (1.14)
  waiting for transfers between devices: 233 us -> 269 us
  starting transfers between devices: 36.2 us -> 41.5 us
    all_to_all x1, waiting for transfers between devices: 0.15 us -> 43.8 us  [per_device(): lax.all_to_all(x_buf, 'expert', split_axis=0, concat_axis=0, tiled=True)]
    all_gather x1 -> x0, waiting for transfers between devices: 43.1 us -> none  [per_device(): lax.all_gather(up_w[0], 'dp', axis=0, tiled=True)]
    all_to_all x0 -> x1, waiting for transfers between devices: none -> 38.6 us  [per_device(): lax.all_to_all(jnp.stack([up_w[0]] * lax.axis_size('dp')), 'dp', 0, 0)]
    all_to_all x0 -> x1, starting transfers between devices: none -> 5.54 us  [per_device(): lax.all_to_all(jnp.stack([up_w[0]] * lax.axis_size('dp')), 'dp', 0, 0)]
    all_to_all x1, waiting for transfers between devices: 34.1 us -> 29.5 us  [per_device(): lax.all_to_all(expert_forward(received, w_gate, w_up, w_down), 'expert',...]
    another operation x0 -> x1, other arithmetic: none -> 4.3 us  [per_device(): jnp.stack([up_w[0]] * lax.axis_size('dp'))]
  transfers between devices with their start and end apart: 11 -> 11, of which waited for: 7 -> 7; matrix products, arithmetic and copies ran while one was open for 17% -> 15% of each run, Pallas kernels for 0% -> 0%
where the time goes in v1:
time: 397 us; the launch traced here: 396 us
  waiting for transfers between devices  269 us (68%)
  starting transfers between devices  41.5 us (10%)
  matrix products  33.5 us (8%)
  local copies, waits for them, and re-layouts  21.2 us (5%)
  other arithmetic  16.8 us (4%)
  between operations  14 us (4%)
    all_to_all x1, waiting for transfers between devices, per_device(): lax.all_to_all(f_buf, 'expert', split_axis=0, concat_axis=0, tiled=True)  52.5 us
    all_to_all x1, waiting for transfers between devices, per_device(): lax.all_to_all(z_buf, 'expert', split_axis=0, concat_axis=0, tiled=True)  49.6 us
    all_to_all x1, waiting for transfers between devices, per_device(): lax.all_to_all(x_buf, 'expert', split_axis=0, concat_axis=0, tiled=True)  43.8 us
    all_to_all x1, waiting for transfers between devices, per_device(): lax.all_to_all(back, 'expert', split_axis=0, concat_axis=0, tiled=True)  41.5 us
    all_to_all x1, waiting for transfers between devices, per_device(): lax.all_to_all(jnp.stack([up_w[0]] * lax.axis_size('dp')), 'dp', 0, 0)  38.6 us
    all_to_all x1, waiting for transfers between devices, per_device(): lax.all_to_all(expert_forward(received, w_gate, w_up, w_down), 'expert',...  29.5 us
    ppermute x2, waiting for transfers between devices, shifted(): return lax.ppermute(block, axis, route)  12.3 us
    all_to_all x1, starting transfers between devices, per_device(): lax.all_to_all(f_buf, 'expert', split_axis=0, concat_axis=0, tiled=True)  10.6 us
  transfers between devices with their start and end apart: 11, of which 7 were waited for; matrix products, arithmetic and copies ran while one was open for 15% of the time, Pallas kernels for 0%

profile of v1, /device:TPU:1, one launch (start us, length us, event | category | flops | bytes accessed | tf_op | source)
XLA Modules:
  0.0 396.2 jit_solution(2660501097905261238)
XLA Ops:
  7.2 0.0 copy-start
  7.2 4.3 %pad_maximum_fusion = bf16[2,1792,512]{2,1,0:T(8,128)(2,1)} fusion(bf16[1,1792,512]{2,1,0:T(8,128)(2,1)} %param.18), kind=kLoop, calls=%fused_computation.11 | loop fusion | flops 1835008 | bytes 5505024 | tf_op jit(solution)/shard_map/stack | solution.py:78
  11.5 5.5 %all-to-all-start.1 = ((bf16[2,1792,512]{2,1,0:T(8,128)(2,1)}), bf16[2,1792,512]{2,1,0:T(8,128)(2,1)}, u32[]{:S(2)}, u32[]{:S(2)}) async-start(bf16[2,1792,512]{2,1,0:T(8,128)(2,1)} %pad_maximum_fusion), calls=%async_computation.1 | async-start | bytes 7340032 | tf_op jit(solution)/shard_map/all_to_all | solution.py:78
  17.0 0.0 copy-done.11
  17.0 0.1 fusion.32
  17.1 0.2 reduce_window_sum.17
  17.3 0.2 select_reduce_fusion.1
  17.5 2.2 scatter_custom_fusion
  19.7 38.6 %all-to-all-done.1 = bf16[2,1792,512]{2,1,0:T(8,128)(2,1)} async-done(((bf16[2,1792,512]{2,1,0:T(8,128)(2,1)}), bf16[2,1792,512]{2,1,0:T(8,128)(2,1)}, u32[]{:S(2)}, u32[]{:S(2)}) %all-to-all-start.1) | async-done | bytes 3670048 | tf_op jit(solution)/shard_map/all_to_all | solution.py:78
  58.3 1.6 broadcast_in_dim.8
  59.9 10.6 %all-to-all-start = ((bf16[8,40,3584]{2,1,0:T(8,128)(2,1)}), bf16[8,40,3584]{2,1,0:T(8,128)(2,1)}, u32[]{:S(2)}, u32[]{:S(2)}) async-start(bf16[8,40,3584]{2,1,0:T(8,128)(2,1)} %bitcast.7), calls=%async_computation | async-start | bytes 4587520 | tf_op jit(solution)/shard_map/all_to_all | solution.py:97
  70.5 0.0 all-gather.5.cloned.1.call-start
  70.5 0.7 all-gather.5.cloned.1.call-update
  71.2 0.1 fusion.31
  71.3 0.2 reduce_window_sum.18
  71.5 0.2 select_reduce_fusion
  71.7 2.3 scatter_custom_fusion.1
  74.0 52.5 %all-to-all-done = bf16[8,40,3584]{2,1,0:T(8,128)(2,1)} async-done(((bf16[8,40,3584]{2,1,0:T(8,128)(2,1)}), bf16[8,40,3584]{2,1,0:T(8,128)(2,1)}, u32[]{:S(2)}, u32[]{:S(2)}) %all-to-all-start) | async-done | bytes 2293792 | tf_op jit(solution)/shard_map/all_to_all | solution.py:97
  126.5 1.7 broadcast_in_dim.9
  128.1 4.4 %all-to-all-start.3 = ((bf16[8,40,3584]{2,1,0:T(8,128)(2,1)}), bf16[8,40,3584]{2,1,0:T(8,128)(2,1)}, u32[]{:S(2)}, u32[]{:S(2)}) async-start(bf16[8,40,3584]{2,1,0:T(8,128)(2,1)} %bitcast.23), calls=%async_computation.3 | async-start | bytes 4587520 | tf_op jit(solution)/shard_map/all_to_all | solution.py:107
  132.5 0.0 all-gather.7.cloned.1.call-start
  132.6 0.7 all-gather.7.cloned.1.call-update
  133.3 2.2 scatter_custom_fusion.2
  135.5 49.6 %all-to-all-done.3 = bf16[8,40,3584]{2,1,0:T(8,128)(2,1)} async-done(((bf16[8,40,3584]{2,1,0:T(8,128)(2,1)}), bf16[8,40,3584]{2,1,0:T(8,128)(2,1)}, u32[]{:S(2)}, u32[]{:S(2)}) %all-to-all-start.3) | async-done | bytes 2293792 | tf_op jit(solution)/shard_map/all_to_all | solution.py:107
  185.0 1.5 broadcast_in_dim.10
  186.6 4.8 %all-to-all-start.4 = ((bf16[8,40,3584]{2,1,0:T(8,128)(2,1)}), bf16[8,40,3584]{2,1,0:T(8,128)(2,1)S(1)}, u32[]{:S(2)}, u32[]{:S(2)}) async-start(bf16[8,40,3584]{2,1,0:T(8,128)(2,1)} %bitcast.27), calls=%async_computation.4 | async-start | bytes 4587520 | tf_op jit(solution)/shard_map/all_to_all | solution.py:106
  191.4 0.0 all-gather.5.cloned.1.call-done
  191.4 4.1 %fusion.8 = f32[320,512]{1,0:T(8,128)S(1)} fusion(bf16[320,3584]{1,0:T(8,128)(2,1)} %bitcast.8, bf16[1,3584,512]{2,1,0:T(8,128)(2,1)} %all-gather.5.cloned.1.call-done), kind=kOutput, calls=%fused_computation.19 | convolution fusion | flops 1174405120 | bytes 6619136 | tf_op jit(solution)/shard_map/dot_general | solution.py:43
  195.5 0.0 all-gather.7.cloned.1.call-done
  195.5 7.9 %convolution_convert_fusion.1 = bf16[320,3584]{1,0:T(8,128)(2,1)} fusion(bf16[1,3584,512]{2,1,0:T(8,128)(2,1)} %all-gather.7.cloned.1.call-done, bf16[320,3584]{1,0:T(8,128)(2,1)} %bitcast.8, bf16[3584,512]{1,0:T(8,128)(2,1)} %bitcast.10, f32[320,512]{1,0:T(8,128)S(1)} %fusion.8), kind=kOutput, calls=%fused_computation.8 | convolution fusion | flops 2350940160 | bytes 12582912 | tf_op jit(solution)/shard_map/dot_general | solution.py:46
  203.5 43.8 %all-to-all-done.4 = bf16[8,40,3584]{2,1,0:T(8,128)(2,1)S(1)} async-done(((bf16[8,40,3584]{2,1,0:T(8,128)(2,1)}), bf16[8,40,3584]{2,1,0:T(8,128)(2,1)S(1)}, u32[]{:S(2)}, u32[]{:S(2)}) %all-to-all-start.4) | async-done | bytes 2293792 | tf_op jit(solution)/shard_map/all_to_all | solution.py:106
  247.3 1.4 copy-done.7
  248.6 3.6 all-to-all-start.2
  252.3 0.2 reduce-scatter.2.cloned.1.call-start
  252.5 4.2 %fusion.1 = f32[320,512]{1,0:T(8,128)S(1)} fusion(bf16[320,3584]{1,0:T(8,128)(2,1)} %bitcast.24, bf16[1,3584,512]{2,1,0:T(8,128)(2,1)} %all-gather.7.cloned.1.call-done), kind=kOutput, calls=%fused_computation.12 | convolution fusion | flops 1174405120 | bytes 6619136 | tf_op jit(solution)/shard_map/dot_general | solution.py:60
  256.7 0.3 copy-done.8
  257.0 1.3 fusion.6
  258.3 0.0 copy-start.9
  258.4 0.8 copy-done.9
  259.2 3.5 fusion.18
  262.7 4.0 %convolution_convert_fusion = bf16[3584,512]{1,0:T(8,128)(2,1)} fusion(bf16[320,3584]{1,0:T(8,128)(2,1)S(1)} %bitcast.93, bf16[320,512]{1,0:T(8,128)(2,1)S(1)} %fusion.18), kind=kOutput, calls=%fused_computation.5 | convolution fusion | flops 1176240128 | bytes 6291456 | tf_op jit(solution)/shard_map/dot_general | solution.py:122
  266.7 0.0 reduce-scatter.2.cloned.1.call-update
  266.8 0.0 copy-start.10
  266.8 3.5 fusion.4
  270.3 0.0 copy-done.10
  270.3 4.9 %fusion = bf16[320,3584]{1,0:T(8,128)(2,1)} fusion(f32[320,3584]{1,0:T(8,128)S(1)} %fusion.4, bf16[3584,512]{1,0:T(8,128)(2,1)} %bitcast.10, f32[320,512]{1,0:T(8,128)S(1)} %fusion.1, f32[320,512]{1,0:T(8,128)S(1)} %copy-done.10), kind=kOutput, calls=%fused_computation.7 | convolution fusion | flops 1177681920 | bytes 11862016 | tf_op jit(solution)/shard_map/dot_general | solution.py:65
  275.1 29.5 %all-to-all-done.2 = bf16[8,40,3584]{2,1,0:T(8,128)(2,1)S(1)} async-done(((bf16[8,40,3584]{2,1,0:T(8,128)(2,1)}), bf16[8,40,3584]{2,1,0:T(8,128)(2,1)S(1)}, u32[]{:S(2)}, u32[]{:S(2)}) %all-to-all-start.2) | async-done | bytes 2293792 | tf_op jit(solution)/shard_map/all_to_all | solution.py:98
  304.7 1.5 copy-done.2
  306.2 4.8 %all-to-all-start.5 = ((bf16[8,40,3584]{2,1,0:T(8,128)(2,1)}), bf16[8,40,3584]{2,1,0:T(8,128)(2,1)}, u32[]{:S(2)}, u32[]{:S(2)}) async-start(bf16[8,40,3584]{2,1,0:T(8,128)(2,1)} %bitcast.29), calls=%async_computation.5 | async-start | bytes 4587520 | tf_op jit(solution)/shard_map/all_to_all | solution.py:110
  311.0 2.4 convert_reduce_fusion.1
  313.4 0.0 copy-start.6
  313.4 0.0 copy-start.14
  313.4 2.4 gather_fusion
  315.9 2.7 fusion.14
  318.6 4.5 %collective-permute-start = (bf16[1,128,3584]{2,1,0:T(8,128)(2,1)}, bf16[1,128,3584]{2,1,0:T(8,128)(2,1)}, u32[]{:S(2)}, u32[]{:S(2)}) collective-permute-start(bf16[1,128,3584]{2,1,0:T(8,128)(2,1)} %fusion.14), channel_id=1, source_target_pairs={{240,0},{0,16},{16,32},{32,48},{48,64},{64,80},{80,96},{96,112},{1... | collective-permute-start | bytes 2752520 | tf_op jit(solution)/shard_map/ppermute | solution.py:12
  323.1 41.5 %all-to-all-done.5 = bf16[8,40,3584]{2,1,0:T(8,128)(2,1)} async-done(((bf16[8,40,3584]{2,1,0:T(8,128)(2,1)}), bf16[8,40,3584]{2,1,0:T(8,128)(2,1)}, u32[]{:S(2)}, u32[]{:S(2)}) %all-to-all-start.5) | async-done | bytes 2293792 | tf_op jit(solution)/shard_map/all_to_all | solution.py:110
  364.6 2.3 convert_reduce_fusion
  366.9 2.4 gather_fusion.1
  369.3 2.0 fusion.10
  371.3 3.0 collective-permute-start.1
  374.3 0.0 collective-permute-done
  374.3 12.3 %collective-permute-done.1 = bf16[1,128,3584]{2,1,0:T(8,128)(2,1)S(1)} collective-permute-done((bf16[1,128,3584]{2,1,0:T(8,128)(2,1)S(1)}, bf16[1,128,3584]{2,1,0:T(8,128)(2,1)S(1)}, u32[]{:S(2)}, u32[]{:S(2)}) %collective-permute-start.1) | collective-permute-done | bytes 917536 | tf_op jit(solution)/shard_map/ppermute | solution.py:12
  386.6 2.2 copy.15
  388.7 0.9 copy.16
  (24 shorter events, 0.1 us)
Async XLA Ops:
  7.2 126.1 %copy-start = (bf16[1,128,3584]{2,1,0:T(8,128)(2,1)S(1)}, bf16[1,128,3584]{2,1,0:T(8,128)(2,1)}, u32[]{:S(2)}) copy-start(bf16[1,128,3584]{2,1,0:T(8,128)(2,1)} %param.13) | copy-start | bytes 2752516
  11.5 5.6 %copy-start.11 = (s32[1,128,1]{1,2,0:T(1,128)S(1)}, s32[1,128,1]{1,2,0:T(1,128)}, u32[]{:S(2)}) copy-start(s32[1,128,1]{1,2,0:T(1,128)} %param.11) | copy-start | bytes 1540
  11.5 6.0 %copy-start.5 = (bf16[1,128,3584]{2,1,0:T(8,128)(2,1)S(1)}, bf16[1,128,3584]{2,1,0:T(8,128)(2,1)}, u32[]{:S(2)}) copy-start(bf16[1,128,3584]{2,1,0:T(8,128)(2,1)} %param.10) | copy-start | bytes 2752516
  11.5 46.8 %all-to-all-start.1 = ((bf16[2,1792,512]{2,1,0:T(8,128)(2,1)}), bf16[2,1792,512]{2,1,0:T(8,128)(2,1)}, u32[]{:S(2)}, u32[]{:S(2)}) async-start(bf16[2,1792,512]{2,1,0:T(8,128)(2,1)} %pad_maximum_fusion), calls=%async_computation.1 | async-start | bytes 7340032 | tf_op jit(solution)/shard_map/all_to_all | solution.py:78
  59.9 11.3 %copy-start.12 = (s32[1,128,1]{1,2,0:T(1,128)S(1)}, s32[1,128,1]{1,2,0:T(1,128)}, u32[]{:S(2)}) copy-start(s32[1,128,1]{1,2,0:T(1,128)} %param.15) | copy-start | bytes 1540
  59.9 11.8 %copy-start.3 = (bf16[1,128,3584]{2,1,0:T(8,128)(2,1)S(1)}, bf16[1,128,3584]{2,1,0:T(8,128)(2,1)}, u32[]{:S(2)}) copy-start(bf16[1,128,3584]{2,1,0:T(8,128)(2,1)} %param.14) | copy-start | bytes 2752516
  59.9 11.8 %copy-start.13 = (f32[1,128,1]{1,2,0:T(1,128)S(1)}, f32[1,128,1]{1,2,0:T(1,128)}, u32[]{:S(2)}) copy-start(f32[1,128,1]{1,2,0:T(1,128)} %param.16) | copy-start | bytes 1540
  59.9 66.5 %all-to-all-start = ((bf16[8,40,3584]{2,1,0:T(8,128)(2,1)}), bf16[8,40,3584]{2,1,0:T(8,128)(2,1)}, u32[]{:S(2)}, u32[]{:S(2)}) async-start(bf16[8,40,3584]{2,1,0:T(8,128)(2,1)} %bitcast.7), calls=%async_computation | async-start | bytes 4587520 | tf_op jit(solution)/shard_map/all_to_all | solution.py:97
  70.5 120.9 %all-gather.5.cloned.1.call-start = ((), (), s32[]{:S(2)}) async-start(), calls=%async_computation.8 | async-start | bytes 5505024 | tf_op jit(solution)/shard_map/all_gather | solution.py:76
  128.1 56.9 %all-to-all-start.3 = ((bf16[8,40,3584]{2,1,0:T(8,128)(2,1)}), bf16[8,40,3584]{2,1,0:T(8,128)(2,1)}, u32[]{:S(2)}, u32[]{:S(2)}) async-start(bf16[8,40,3584]{2,1,0:T(8,128)(2,1)} %bitcast.23), calls=%async_computation.3 | async-start | bytes 4587520 | tf_op jit(solution)/shard_map/all_to_all | solution.py:107
  132.5 63.0 %all-gather.7.cloned.1.call-start = ((), (), s32[]{:S(2)}) async-start(), calls=%async_computation.9 | async-start | bytes 5505024 | tf_op jit(solution)/shard_map/all_gather | solution.py:80
  186.6 60.7 %all-to-all-start.4 = ((bf16[8,40,3584]{2,1,0:T(8,128)(2,1)}), bf16[8,40,3584]{2,1,0:T(8,128)(2,1)S(1)}, u32[]{:S(2)}, u32[]{:S(2)}) async-start(bf16[8,40,3584]{2,1,0:T(8,128)(2,1)} %bitcast.27), calls=%async_computation.4 | async-start | bytes 4587520 | tf_op jit(solution)/shard_map/all_to_all | solution.py:106
  247.3 1.4 copy-start.7
  248.6 56.0 %all-to-all-start.2 = ((bf16[8,40,3584]{2,1,0:T(8,128)(2,1)}), bf16[8,40,3584]{2,1,0:T(8,128)(2,1)S(1)}, u32[]{:S(2)}, u32[]{:S(2)}) async-start(bf16[8,40,3584]{2,1,0:T(8,128)(2,1)} %bitcast.90), calls=%async_computation.2 | async-start | bytes 4587520 | tf_op jit(solution)/shard_map/all_to_all | solution.py:98
  252.3 134.3 %reduce-scatter.2.cloned.1.call-start = ((), (), s32[]{:S(2)}) async-start(), calls=%async_computation.7 | async-start | bytes 5505024 | tf_op jit(solution)/shard_map/reduce_scatter | solution.py:121
  252.5 4.2 %copy-start.4 = (bf16[1,3584,512]{2,1,0:T(8,128)(2,1)S(1)}, bf16[1,3584,512]{2,1,0:T(8,128)(2,1)}, u32[]{:S(2)}) copy-start(bf16[1,3584,512]{2,1,0:T(8,128)(2,1)} %all-gather.5.cloned.1.call-done) | copy-start | bytes 11010052
  252.5 4.5 %copy-start.8 = (bf16[8,40,3584]{2,1,0:T(8,128)(2,1)S(1)}, bf16[8,40,3584]{2,1,0:T(8,128)(2,1)}, u32[]{:S(2)}) copy-start(bf16[8,40,3584]{2,1,0:T(8,128)(2,1)} %copy-done.7) | copy-start | bytes 6881284
  258.3 0.8 copy-start.9
  266.8 3.5 copy-start.10
  304.7 1.5 copy-start.2
  306.2 58.5 %all-to-all-start.5 = ((bf16[8,40,3584]{2,1,0:T(8,128)(2,1)}), bf16[8,40,3584]{2,1,0:T(8,128)(2,1)}, u32[]{:S(2)}, u32[]{:S(2)}) async-start(bf16[8,40,3584]{2,1,0:T(8,128)(2,1)} %bitcast.29), calls=%async_computation.5 | async-start | bytes 4587520 | tf_op jit(solution)/shard_map/all_to_all | solution.py:110
  313.4 2.5 copy-start.6
  313.4 2.4 copy-start.14
  318.6 55.7 %collective-permute-start = (bf16[1,128,3584]{2,1,0:T(8,128)(2,1)}, bf16[1,128,3584]{2,1,0:T(8,128)(2,1)}, u32[]{:S(2)}, u32[]{:S(2)}) collective-permute-start(bf16[1,128,3584]{2,1,0:T(8,128)(2,1)} %fusion.14), channel_id=1, source_target_pairs={{240,0},{0,16},{16,32},{32,48},{48,64},{64,80},{80,96},{96,112},{1... | collective-permute-start | bytes 2752520 | tf_op jit(solution)/shard_map/ppermute | solution.py:12
  369.3 20.3 %copy-start.1 = (bf16[1,128,3584]{2,1,0:T(8,128)(2,1)S(1)}, bf16[1,128,3584]{2,1,0:T(8,128)(2,1)}, u32[]{:S(2)}) copy-start(bf16[1,128,3584]{2,1,0:T(8,128)(2,1)} %param.13) | copy-start | bytes 2752516
  371.3 15.2 %collective-permute-start.1 = (bf16[1,128,3584]{2,1,0:T(8,128)(2,1)S(1)}, bf16[1,128,3584]{2,1,0:T(8,128)(2,1)S(1)}, u32[]{:S(2)}, u32[]{:S(2)}) collective-permute-start(bf16[1,128,3584]{2,1,0:T(8,128)(2,1)S(1)} %fusion.10), channel_id=1, source_target_pairs={{16,0},{32,16},{48,32},{64,48},{80,64},{96,80},{112,96},{128,112},... | collective-permute-start | bytes 2752520 | tf_op jit(solution)/shard_map/ppermute | solution.py:12
Sparse Core Ops, SparseCore 0:
  73.1 58.7 all-gather.4
  135.2 57.3 all-gather.6
  266.9 55.3 reduce-scatter.1
